TPU v7x, 32 devices: a whole 2x2x4 slice. The times are simulated.
32 devices in a mesh: layer: 8 (over y, x, core), lat: 4 (over z).
Axes of the slice: x: 2, y: 2, z: 4, core: 2. Of those that a mesh axis runs over, the one named last changes fastest.
Arguments:
- source: float32 [8, 2, 1536, 128], P('layer', None, 'lat'), may hold values from -6 to 6
- wavenumber: float32 [8, 1536, 128], P('layer', 'lat'), may hold values from 0.1 to 1
- green_down: bfloat16 [8, 2, 1536, 3072], P('layer', None, 'lat'), may hold values from -0.109375 to 0.109375
- green_up: bfloat16 [8, 2, 1536, 3072], P('layer', None, 'lat'), may hold values from -0.109375 to 0.109375
Outputs:
- down_trace: float32 [8, 2, 1536, 128], P('layer', None, 'lat')
- up_trace: float32 [8, 2, 1536, 128], P('layer', None, 'lat')
All inputs are finite; a program needn't handle non-finite values.
Results may differ from a plain program's by a relative error of at most 0.017.
Values may be sent and summed in bfloat16 or wider, within the bound.
A program may use at most 64 MiB of HBM per device.

v0:
```python
import jax
import jax.numpy as jnp
from jax import lax
from jax.sharding import PartitionSpec as P

RELAX = 4


relax_weight = 0.8
damping = 0.5


def padded_2(block, sides, width):
    for axis, dim in sides:
        count = lax.axis_size(axis)
        forward = [(i, i + 1) for i in range(count - 1)]
        backward = [(target, source) for source, target in forward]
        low = lax.ppermute(
            lax.slice_in_dim(block, block.shape[dim] - width, None, axis=dim), axis, forward
        )
        high = lax.ppermute(lax.slice_in_dim(block, 0, width, axis=dim), axis, backward)
        block = jnp.concatenate([low, block, high], axis=dim)
    return block


def shifted(block, axis, distance):
    devices = range(lax.axis_size(axis))
    route = [(i - distance, i) for i in devices if i - distance in devices]
    return lax.ppermute(block, axis, route)


def relax_step(field, lateral_pad, forcing, diag_real, diag_imag, inverse_real, inverse_imag):
    along = jnp.pad(field, ((0, 0), (0, 0), (1, 1)))
    beside = lateral_pad[:, 2:] + lateral_pad[:, :-2] + along[:, :, 2:] + along[:, :, :-2]
    apply_real = diag_real * field[0] - diag_imag * field[1] - beside[0]
    apply_imag = diag_real * field[1] + diag_imag * field[0] - beside[1]
    res_real = forcing[0] - apply_real
    res_imag = forcing[1] - apply_imag
    step_real = res_real * inverse_real - res_imag * inverse_imag
    step_imag = res_real * inverse_imag + res_imag * inverse_real
    return field + relax_weight * jnp.stack([step_real, step_imag], 0)


def coefficients(wave_sq):
    diag_real = 4.0 - wave_sq
    diag_imag = damping * wave_sq
    denom = diag_real * diag_real + diag_imag * diag_imag
    return (diag_real, diag_imag, diag_real / denom, -diag_imag / denom)


def add_block(flat, width, total, piece):
    count = piece.shape[1]
    for part in range(2):
        columns = lax.dynamic_slice_in_dim(flat, part * width, count, 1)
        total = total + jnp.dot(columns, piece[part], preferred_element_type=jnp.float32)
    return total


def local(source, wavenumber, green_down, green_up):
    forcing = source[0]
    wave_sq = wavenumber[0]
    slab = forcing.shape[1]
    rows_here = forcing.shape[2]
    width = slab * lax.axis_size("lat")
    diag_real, diag_imag, inverse_real, inverse_imag = coefficients(wave_sq)
    field = jnp.zeros_like(forcing)
    for sweep in range(RELAX):
        padded = padded_2(field.astype(jnp.bfloat16), (("lat", 1),), 1).astype(field.dtype)
        field = relax_step(field, padded, forcing, diag_real, diag_imag, inverse_real, inverse_imag)
    traces = field
    flat_down = green_down[0].reshape(2 * slab, 2 * width)
    flat_up = green_up[0].reshape(2 * slab, 2 * width)
    empty = jnp.zeros((2 * slab, rows_here), jnp.float32)
    turns = lax.axis_size("layer") - 1

    def fold_pair(totals, pieces):
        return (
            add_block(flat_down, width, totals[0], pieces[0]),
            add_block(flat_up, width, totals[1], pieces[1]),
        )

    def pair_turn(step, pair):
        below = shifted(pair[0].astype(jnp.bfloat16), "layer", 1)
        above = shifted(pair[1].astype(jnp.bfloat16), "layer", -1)
        down_sum, up_sum = fold_pair(
            (empty, empty),
            (
                lax.all_gather(below, "lat", axis=1, tiled=True),
                lax.all_gather(above, "lat", axis=1, tiled=True),
            ),
        )
        return (
            traces + down_sum.reshape(2, slab, rows_here),
            traces + up_sum.reshape(2, slab, rows_here),
        )

    down_trace, up_trace = lax.fori_loop(0, turns, pair_turn, (traces, traces))
    return (down_trace[None], up_trace[None])


def solution(mesh):
    return jax.shard_map(
        local,
        mesh=mesh,
        in_specs=(
            P("layer", None, "lat", None),
            P("layer", "lat", None),
            P("layer", None, "lat", None),
            P("layer", None, "lat", None),
        ),
        out_specs=(P("layer", None, "lat", None), P("layer", None, "lat", None)),
        check_vma=False,
    )
```

profile of v0, /device:TPU:0, one launch (start us, length us, event | category | flops | bytes accessed | tf_op | source)
XLA Modules:
  0.0 364.6 jit_solution(12718919259994259636)
XLA Ops:
  2.1 5.6 %collective-permute-start.2 = (bf16[2,1,128]{2,1,0:T(2,128)(2,1)S(1)}, bf16[2,1,128]{2,1,0:T(2,128)(2,1)S(1)}, u32[]{:S(2)}, u32[]{:S(2)}) collective-permute-start(bf16[2,1,128]{2,1,0:T(2,128)(2,1)S(1)} %slice.147), channel_id=1, source_target_pairs={{0,1},{1,2},{2,3},{4,5},{5,6},{6,7},{8,9},{9,10},{10,11},{12,13},{... | collective-permute-start | bytes 1544 | tf_op jit(solution)/shard_map/ppermute | solution.py:18
  10.5 4.2 %collective-permute-start.4 = (bf16[2,1,128]{2,1,0:T(2,128)(2,1)S(1)}, bf16[2,1,128]{2,1,0:T(2,128)(2,1)S(1)}, u32[]{:S(2)}, u32[]{:S(2)}) collective-permute-start(bf16[2,1,128]{2,1,0:T(2,128)(2,1)S(1)} %get-tuple-element.72), channel_id=1, source_target_pairs={{0,1},{1,2},{2,3},{4,5},{5,6},{6,7},{8,9},{9,10},{10,11},{12,13},{... | collective-permute-start | bytes 1544 | tf_op jit(solution)/shard_map/ppermute | solution.py:18
  16.0 4.2 %collective-permute-done.5 = bf16[2,1,128]{2,1,0:T(2,128)(2,1)S(1)} collective-permute-done((bf16[2,1,128]{2,1,0:T(2,128)(2,1)S(1)}, bf16[2,1,128]{2,1,0:T(2,128)(2,1)S(1)}, u32[]{:S(2)}, u32[]{:S(2)}) %collective-permute-start.5) | collective-permute-done | bytes 544 | tf_op jit(solution)/shard_map/ppermute | solution.py:21
  20.8 3.9 %collective-permute-start.6 = (bf16[2,1,128]{2,1,0:T(2,128)(2,1)S(1)}, bf16[2,1,128]{2,1,0:T(2,128)(2,1)S(1)}, u32[]{:S(2)}, u32[]{:S(2)}) collective-permute-start(bf16[2,1,128]{2,1,0:T(2,128)(2,1)S(1)} %get-tuple-element.70), channel_id=1, source_target_pairs={{0,1},{1,2},{2,3},{4,5},{5,6},{6,7},{8,9},{9,10},{10,11},{12,13},{... | collective-permute-start | bytes 1544 | tf_op jit(solution)/shard_map/ppermute | solution.py:18
  26.1 4.2 %collective-permute-done.7 = bf16[2,1,128]{2,1,0:T(2,128)(2,1)S(1)} collective-permute-done((bf16[2,1,128]{2,1,0:T(2,128)(2,1)S(1)}, bf16[2,1,128]{2,1,0:T(2,128)(2,1)S(1)}, u32[]{:S(2)}, u32[]{:S(2)}) %collective-permute-start.7) | collective-permute-done | bytes 544 | tf_op jit(solution)/shard_map/ppermute | solution.py:21
  30.9 3.5 collective-permute-start.8
  35.7 4.2 %collective-permute-done.9 = bf16[2,1,128]{2,1,0:T(2,128)(2,1)S(1)} collective-permute-done((bf16[2,1,128]{2,1,0:T(2,128)(2,1)S(1)}, bf16[2,1,128]{2,1,0:T(2,128)(2,1)S(1)}, u32[]{:S(2)}, u32[]{:S(2)}) %collective-permute-start.9) | collective-permute-done | bytes 544 | tf_op jit(solution)/shard_map/ppermute | solution.py:21
  40.5 323.1 %while.12 = (s32[]{:T(128)}, f32[2,384,128]{2,1,0:T(8,128)S(1)}, f32[2,384,128]{2,1,0:T(8,128)S(1)}, bf16[768,3072]{1,0:T(8,128)(2,1)}, f32[2,384,128]{2,1,0:T(8,128)S(1)}, /*index=5*/bf16[768,3072]{1,0:T(8,128)(2,1)}, s32[]{:T(128)}) while((s32[]{:T(128)}, f32[2,384,128]{2,1,0:T(8,128)S(1)}, f32[2,384,128]{2,1,0:T(8,128)S(1)}, ...), condition=%wide.region_1.2_spmd, body=%wide.region_0.1_spmd.sunk | while | flops 1208549376 | bytes 53084392 | solution.py:97
  41.9 3.2 collective-permute-start.1
  45.1 17.8 %all_gather.8 = bf16[2,1536,128]{2,1,0:T(8,128)(2,1)S(1)} all-gather(bf16[2,384,128]{2,1,0:T(8,128)(2,1)S(1)} %collective-permute-done), channel_id=1, replica_groups=mesh['layer'=8,'lat'=4] {'lat'}, dimensions={1}, use_global_device_ids=true | all-gather | bytes 983040 | tf_op jit(solution)/shard_map/while/body/eval_jaxpr/all_gather | solution.py:89
  66.3 18.0 %all_gather.9 = bf16[2,1536,128]{2,1,0:T(8,128)(2,1)S(1)} all-gather(bf16[2,384,128]{2,1,0:T(8,128)(2,1)S(1)} %collective-permute-done.1), channel_id=1, replica_groups=mesh['layer'=8,'lat'=4] {'lat'}, dimensions={1}, use_global_device_ids=true | all-gather | bytes 983040 | tf_op jit(solution)/shard_map/while/body/eval_jaxpr/all_gather | solution.py:88
  90.5 18.1 %all_gather.8 = bf16[2,1536,128]{2,1,0:T(8,128)(2,1)S(1)} all-gather(bf16[2,384,128]{2,1,0:T(8,128)(2,1)S(1)} %collective-permute-done), channel_id=1, replica_groups=mesh['layer'=8,'lat'=4] {'lat'}, dimensions={1}, use_global_device_ids=true | all-gather | bytes 983040 | tf_op jit(solution)/shard_map/while/body/eval_jaxpr/all_gather | solution.py:89
  112.1 18.5 %all_gather.9 = bf16[2,1536,128]{2,1,0:T(8,128)(2,1)S(1)} all-gather(bf16[2,384,128]{2,1,0:T(8,128)(2,1)S(1)} %collective-permute-done.1), channel_id=1, replica_groups=mesh['layer'=8,'lat'=4] {'lat'}, dimensions={1}, use_global_device_ids=true | all-gather | bytes 983040 | tf_op jit(solution)/shard_map/while/body/eval_jaxpr/all_gather | solution.py:88
  136.8 18.0 %all_gather.8 = bf16[2,1536,128]{2,1,0:T(8,128)(2,1)S(1)} all-gather(bf16[2,384,128]{2,1,0:T(8,128)(2,1)S(1)} %collective-permute-done), channel_id=1, replica_groups=mesh['layer'=8,'lat'=4] {'lat'}, dimensions={1}, use_global_device_ids=true | all-gather | bytes 983040 | tf_op jit(solution)/shard_map/while/body/eval_jaxpr/all_gather | solution.py:89
  158.2 18.8 %all_gather.9 = bf16[2,1536,128]{2,1,0:T(8,128)(2,1)S(1)} all-gather(bf16[2,384,128]{2,1,0:T(8,128)(2,1)S(1)} %collective-permute-done.1), channel_id=1, replica_groups=mesh['layer'=8,'lat'=4] {'lat'}, dimensions={1}, use_global_device_ids=true | all-gather | bytes 983040 | tf_op jit(solution)/shard_map/while/body/eval_jaxpr/all_gather | solution.py:88
  183.2 18.4 %all_gather.8 = bf16[2,1536,128]{2,1,0:T(8,128)(2,1)S(1)} all-gather(bf16[2,384,128]{2,1,0:T(8,128)(2,1)S(1)} %collective-permute-done), channel_id=1, replica_groups=mesh['layer'=8,'lat'=4] {'lat'}, dimensions={1}, use_global_device_ids=true | all-gather | bytes 983040 | tf_op jit(solution)/shard_map/while/body/eval_jaxpr/all_gather | solution.py:89
  205.0 18.5 %all_gather.9 = bf16[2,1536,128]{2,1,0:T(8,128)(2,1)S(1)} all-gather(bf16[2,384,128]{2,1,0:T(8,128)(2,1)S(1)} %collective-permute-done.1), channel_id=1, replica_groups=mesh['layer'=8,'lat'=4] {'lat'}, dimensions={1}, use_global_device_ids=true | all-gather | bytes 983040 | tf_op jit(solution)/shard_map/while/body/eval_jaxpr/all_gather | solution.py:88
  229.8 18.4 %all_gather.8 = bf16[2,1536,128]{2,1,0:T(8,128)(2,1)S(1)} all-gather(bf16[2,384,128]{2,1,0:T(8,128)(2,1)S(1)} %collective-permute-done), channel_id=1, replica_groups=mesh['layer'=8,'lat'=4] {'lat'}, dimensions={1}, use_global_device_ids=true | all-gather | bytes 983040 | tf_op jit(solution)/shard_map/while/body/eval_jaxpr/all_gather | solution.py:89
  251.5 18.5 %all_gather.9 = bf16[2,1536,128]{2,1,0:T(8,128)(2,1)S(1)} all-gather(bf16[2,384,128]{2,1,0:T(8,128)(2,1)S(1)} %collective-permute-done.1), channel_id=1, replica_groups=mesh['layer'=8,'lat'=4] {'lat'}, dimensions={1}, use_global_device_ids=true | all-gather | bytes 983040 | tf_op jit(solution)/shard_map/while/body/eval_jaxpr/all_gather | solution.py:88
  273.0 3.2 collective-permute-start.1
  276.2 18.1 %all_gather.8 = bf16[2,1536,128]{2,1,0:T(8,128)(2,1)S(1)} all-gather(bf16[2,384,128]{2,1,0:T(8,128)(2,1)S(1)} %collective-permute-done), channel_id=1, replica_groups=mesh['layer'=8,'lat'=4] {'lat'}, dimensions={1}, use_global_device_ids=true | all-gather | bytes 983040 | tf_op jit(solution)/shard_map/while/body/eval_jaxpr/all_gather | solution.py:89
  297.7 18.4 %all_gather.9 = bf16[2,1536,128]{2,1,0:T(8,128)(2,1)S(1)} all-gather(bf16[2,384,128]{2,1,0:T(8,128)(2,1)S(1)} %collective-permute-done.1), channel_id=1, replica_groups=mesh['layer'=8,'lat'=4] {'lat'}, dimensions={1}, use_global_device_ids=true | all-gather | bytes 983040 | tf_op jit(solution)/shard_map/while/body/eval_jaxpr/all_gather | solution.py:88
  322.3 18.3 %all_gather.8 = bf16[2,1536,128]{2,1,0:T(8,128)(2,1)S(1)} all-gather(bf16[2,384,128]{2,1,0:T(8,128)(2,1)S(1)} %collective-permute-done), channel_id=1, replica_groups=mesh['layer'=8,'lat'=4] {'lat'}, dimensions={1}, use_global_device_ids=true | all-gather | bytes 983040 | tf_op jit(solution)/shard_map/while/body/eval_jaxpr/all_gather | solution.py:89
  344.0 18.1 %all_gather.9 = bf16[2,1536,128]{2,1,0:T(8,128)(2,1)S(1)} all-gather(bf16[2,384,128]{2,1,0:T(8,128)(2,1)S(1)} %collective-permute-done.1), channel_id=1, replica_groups=mesh['layer'=8,'lat'=4] {'lat'}, dimensions={1}, use_global_device_ids=true | all-gather | bytes 983040 | tf_op jit(solution)/shard_map/while/body/eval_jaxpr/all_gather | solution.py:88
  (170 shorter events, 71.2 us)
Async XLA Ops:
  0.7 7.2 %collective-permute-start.3 = (bf16[2,1,128]{2,1,0:T(2,128)(2,1)S(1)}, bf16[2,1,128]{2,1,0:T(2,128)(2,1)S(1)}, u32[]{:S(2)}, u32[]{:S(2)}) collective-permute-start(bf16[2,1,128]{2,1,0:T(2,128)(2,1)S(1)} %slice.147), channel_id=1, source_target_pairs={{1,0},{2,1},{3,2},{5,4},{6,5},{7,6},{9,8},{10,9},{11,10},{13,12},{... | collective-permute-start | bytes 1544 | tf_op jit(solution)/shard_map/ppermute | solution.py:21
  2.1 6.8 %collective-permute-start.2 = (bf16[2,1,128]{2,1,0:T(2,128)(2,1)S(1)}, bf16[2,1,128]{2,1,0:T(2,128)(2,1)S(1)}, u32[]{:S(2)}, u32[]{:S(2)}) collective-permute-start(bf16[2,1,128]{2,1,0:T(2,128)(2,1)S(1)} %slice.147), channel_id=1, source_target_pairs={{0,1},{1,2},{2,3},{4,5},{5,6},{6,7},{8,9},{9,10},{10,11},{12,13},{... | collective-permute-start | bytes 1544 | tf_op jit(solution)/shard_map/ppermute | solution.py:18
  10.5 5.5 %collective-permute-start.4 = (bf16[2,1,128]{2,1,0:T(2,128)(2,1)S(1)}, bf16[2,1,128]{2,1,0:T(2,128)(2,1)S(1)}, u32[]{:S(2)}, u32[]{:S(2)}) collective-permute-start(bf16[2,1,128]{2,1,0:T(2,128)(2,1)S(1)} %get-tuple-element.72), channel_id=1, source_target_pairs={{0,1},{1,2},{2,3},{4,5},{5,6},{6,7},{8,9},{9,10},{10,11},{12,13},{... | collective-permute-start | bytes 1544 | tf_op jit(solution)/shard_map/ppermute | solution.py:18
  14.7 5.5 %collective-permute-start.5 = (bf16[2,1,128]{2,1,0:T(2,128)(2,1)S(1)}, bf16[2,1,128]{2,1,0:T(2,128)(2,1)S(1)}, u32[]{:S(2)}, u32[]{:S(2)}) collective-permute-start(bf16[2,1,128]{2,1,0:T(2,128)(2,1)S(1)} %get-tuple-element.73), channel_id=1, source_target_pairs={{1,0},{2,1},{3,2},{5,4},{6,5},{7,6},{9,8},{10,9},{11,10},{13,12},{... | collective-permute-start | bytes 1544 | tf_op jit(solution)/shard_map/ppermute | solution.py:21
  20.8 5.2 %collective-permute-start.6 = (bf16[2,1,128]{2,1,0:T(2,128)(2,1)S(1)}, bf16[2,1,128]{2,1,0:T(2,128)(2,1)S(1)}, u32[]{:S(2)}, u32[]{:S(2)}) collective-permute-start(bf16[2,1,128]{2,1,0:T(2,128)(2,1)S(1)} %get-tuple-element.70), channel_id=1, source_target_pairs={{0,1},{1,2},{2,3},{4,5},{5,6},{6,7},{8,9},{9,10},{10,11},{12,13},{... | collective-permute-start | bytes 1544 | tf_op jit(solution)/shard_map/ppermute | solution.py:18
  24.8 5.5 %collective-permute-start.7 = (bf16[2,1,128]{2,1,0:T(2,128)(2,1)S(1)}, bf16[2,1,128]{2,1,0:T(2,128)(2,1)S(1)}, u32[]{:S(2)}, u32[]{:S(2)}) collective-permute-start(bf16[2,1,128]{2,1,0:T(2,128)(2,1)S(1)} %get-tuple-element.71), channel_id=1, source_target_pairs={{1,0},{2,1},{3,2},{5,4},{6,5},{7,6},{9,8},{10,9},{11,10},{13,12},{... | collective-permute-start | bytes 1544 | tf_op jit(solution)/shard_map/ppermute | solution.py:21
  30.9 4.8 %collective-permute-start.8 = (bf16[2,1,128]{2,1,0:T(2,128)(2,1)S(1)}, bf16[2,1,128]{2,1,0:T(2,128)(2,1)S(1)}, u32[]{:S(2)}, u32[]{:S(2)}) collective-permute-start(bf16[2,1,128]{2,1,0:T(2,128)(2,1)S(1)} %get-tuple-element.68), channel_id=1, source_target_pairs={{0,1},{1,2},{2,3},{4,5},{5,6},{6,7},{8,9},{9,10},{10,11},{12,13},{... | collective-permute-start | bytes 1544 | tf_op jit(solution)/shard_map/ppermute | solution.py:18
  34.4 5.5 %collective-permute-start.9 = (bf16[2,1,128]{2,1,0:T(2,128)(2,1)S(1)}, bf16[2,1,128]{2,1,0:T(2,128)(2,1)S(1)}, u32[]{:S(2)}, u32[]{:S(2)}) collective-permute-start(bf16[2,1,128]{2,1,0:T(2,128)(2,1)S(1)} %get-tuple-element.69), channel_id=1, source_target_pairs={{1,0},{2,1},{3,2},{5,4},{6,5},{7,6},{9,8},{10,9},{11,10},{13,12},{... | collective-permute-start | bytes 1544 | tf_op jit(solution)/shard_map/ppermute | solution.py:21
  40.6 4.5 %collective-permute-start = (bf16[2,384,128]{2,1,0:T(8,128)(2,1)S(1)}, bf16[2,384,128]{2,1,0:T(8,128)(2,1)S(1)}, u32[]{:S(2)}, u32[]{:S(2)}) collective-permute-start(bf16[2,384,128]{2,1,0:T(8,128)(2,1)S(1)} %convert_element_type.50), channel_id=1, source_target_pairs={{4,0},{8,4},{12,8},{16,12},{20,16},{24,20},{28,24},{5,1},{9,5},{13... | collective-permute-start | bytes 589832 | tf_op jit(solution)/shard_map/while/body/eval_jaxpr/ppermute | solution.py:29
  41.9 24.4 %collective-permute-start.1 = (bf16[2,384,128]{2,1,0:T(8,128)(2,1)S(1)}, bf16[2,384,128]{2,1,0:T(8,128)(2,1)S(1)}, u32[]{:S(2)}, u32[]{:S(2)}) collective-permute-start(bf16[2,384,128]{2,1,0:T(8,128)(2,1)S(1)} %convert_element_type.51), channel_id=1, source_target_pairs={{0,4},{4,8},{8,12},{12,16},{16,20},{20,24},{24,28},{1,5},{5,9},{9,... | collective-permute-start | bytes 589832 | tf_op jit(solution)/shard_map/while/body/eval_jaxpr/ppermute | solution.py:29
  86.0 4.5 %collective-permute-start = (bf16[2,384,128]{2,1,0:T(8,128)(2,1)S(1)}, bf16[2,384,128]{2,1,0:T(8,128)(2,1)S(1)}, u32[]{:S(2)}, u32[]{:S(2)}) collective-permute-start(bf16[2,384,128]{2,1,0:T(8,128)(2,1)S(1)} %convert_element_type.50), channel_id=1, source_target_pairs={{4,0},{8,4},{12,8},{16,12},{20,16},{24,20},{28,24},{5,1},{9,5},{13... | collective-permute-start | bytes 589832 | tf_op jit(solution)/shard_map/while/body/eval_jaxpr/ppermute | solution.py:29
  87.3 24.7 %collective-permute-start.1 = (bf16[2,384,128]{2,1,0:T(8,128)(2,1)S(1)}, bf16[2,384,128]{2,1,0:T(8,128)(2,1)S(1)}, u32[]{:S(2)}, u32[]{:S(2)}) collective-permute-start(bf16[2,384,128]{2,1,0:T(8,128)(2,1)S(1)} %convert_element_type.51), channel_id=1, source_target_pairs={{0,4},{4,8},{8,12},{12,16},{16,20},{20,24},{24,28},{1,5},{5,9},{9,... | collective-permute-start | bytes 589832 | tf_op jit(solution)/shard_map/while/body/eval_jaxpr/ppermute | solution.py:29
  132.3 4.5 %collective-permute-start = (bf16[2,384,128]{2,1,0:T(8,128)(2,1)S(1)}, bf16[2,384,128]{2,1,0:T(8,128)(2,1)S(1)}, u32[]{:S(2)}, u32[]{:S(2)}) collective-permute-start(bf16[2,384,128]{2,1,0:T(8,128)(2,1)S(1)} %convert_element_type.50), channel_id=1, source_target_pairs={{4,0},{8,4},{12,8},{16,12},{20,16},{24,20},{28,24},{5,1},{9,5},{13... | collective-permute-start | bytes 589832 | tf_op jit(solution)/shard_map/while/body/eval_jaxpr/ppermute | solution.py:29
  133.6 24.6 %collective-permute-start.1 = (bf16[2,384,128]{2,1,0:T(8,128)(2,1)S(1)}, bf16[2,384,128]{2,1,0:T(8,128)(2,1)S(1)}, u32[]{:S(2)}, u32[]{:S(2)}) collective-permute-start(bf16[2,384,128]{2,1,0:T(8,128)(2,1)S(1)} %convert_element_type.51), channel_id=1, source_target_pairs={{0,4},{4,8},{8,12},{12,16},{16,20},{20,24},{24,28},{1,5},{5,9},{9,... | collective-permute-start | bytes 589832 | tf_op jit(solution)/shard_map/while/body/eval_jaxpr/ppermute | solution.py:29
  178.7 4.5 %collective-permute-start = (bf16[2,384,128]{2,1,0:T(8,128)(2,1)S(1)}, bf16[2,384,128]{2,1,0:T(8,128)(2,1)S(1)}, u32[]{:S(2)}, u32[]{:S(2)}) collective-permute-start(bf16[2,384,128]{2,1,0:T(8,128)(2,1)S(1)} %convert_element_type.50), channel_id=1, source_target_pairs={{4,0},{8,4},{12,8},{16,12},{20,16},{24,20},{28,24},{5,1},{9,5},{13... | collective-permute-start | bytes 589832 | tf_op jit(solution)/shard_map/while/body/eval_jaxpr/ppermute | solution.py:29
  180.0 43.5 %slice-start = ((s8[4718592]{0:T(1024)(128)(4,1)}), s8[524288]{0:T(1024)(128)(4,1)S(1)}, s32[]{:S(2)}) async-start(s8[4718592]{0:T(1024)(128)(4,1)} %bitcast.59), calls=%async_computation | async-start | bytes 1048576 | tf_op jit(solution)/shard_map/while
  180.0 25.0 %collective-permute-start.1 = (bf16[2,384,128]{2,1,0:T(8,128)(2,1)S(1)}, bf16[2,384,128]{2,1,0:T(8,128)(2,1)S(1)}, u32[]{:S(2)}, u32[]{:S(2)}) collective-permute-start(bf16[2,384,128]{2,1,0:T(8,128)(2,1)S(1)} %convert_element_type.51), channel_id=1, source_target_pairs={{0,4},{4,8},{8,12},{12,16},{16,20},{20,24},{24,28},{1,5},{5,9},{9,... | collective-permute-start | bytes 589832 | tf_op jit(solution)/shard_map/while/body/eval_jaxpr/ppermute | solution.py:29
  225.2 4.5 %collective-permute-start = (bf16[2,384,128]{2,1,0:T(8,128)(2,1)S(1)}, bf16[2,384,128]{2,1,0:T(8,128)(2,1)S(1)}, u32[]{:S(2)}, u32[]{:S(2)}) collective-permute-start(bf16[2,384,128]{2,1,0:T(8,128)(2,1)S(1)} %convert_element_type.50), channel_id=1, source_target_pairs={{4,0},{8,4},{12,8},{16,12},{20,16},{24,20},{28,24},{5,1},{9,5},{13... | collective-permute-start | bytes 589832 | tf_op jit(solution)/shard_map/while/body/eval_jaxpr/ppermute | solution.py:29
  226.5 43.5 %slice-start = ((s8[4718592]{0:T(1024)(128)(4,1)}), s8[524288]{0:T(1024)(128)(4,1)S(1)}, s32[]{:S(2)}) async-start(s8[4718592]{0:T(1024)(128)(4,1)} %bitcast.59), calls=%async_computation | async-start | bytes 1048576 | tf_op jit(solution)/shard_map/while
  226.5 25.0 %collective-permute-start.1 = (bf16[2,384,128]{2,1,0:T(8,128)(2,1)S(1)}, bf16[2,384,128]{2,1,0:T(8,128)(2,1)S(1)}, u32[]{:S(2)}, u32[]{:S(2)}) collective-permute-start(bf16[2,384,128]{2,1,0:T(8,128)(2,1)S(1)} %convert_element_type.51), channel_id=1, source_target_pairs={{0,4},{4,8},{8,12},{12,16},{16,20},{20,24},{24,28},{1,5},{5,9},{9,... | collective-permute-start | bytes 589832 | tf_op jit(solution)/shard_map/while/body/eval_jaxpr/ppermute | solution.py:29
  271.7 4.5 %collective-permute-start = (bf16[2,384,128]{2,1,0:T(8,128)(2,1)S(1)}, bf16[2,384,128]{2,1,0:T(8,128)(2,1)S(1)}, u32[]{:S(2)}, u32[]{:S(2)}) collective-permute-start(bf16[2,384,128]{2,1,0:T(8,128)(2,1)S(1)} %convert_element_type.50), channel_id=1, source_target_pairs={{4,0},{8,4},{12,8},{16,12},{20,16},{24,20},{28,24},{5,1},{9,5},{13... | collective-permute-start | bytes 589832 | tf_op jit(solution)/shard_map/while/body/eval_jaxpr/ppermute | solution.py:29
  273.0 24.7 %collective-permute-start.1 = (bf16[2,384,128]{2,1,0:T(8,128)(2,1)S(1)}, bf16[2,384,128]{2,1,0:T(8,128)(2,1)S(1)}, u32[]{:S(2)}, u32[]{:S(2)}) collective-permute-start(bf16[2,384,128]{2,1,0:T(8,128)(2,1)S(1)} %convert_element_type.51), channel_id=1, source_target_pairs={{0,4},{4,8},{8,12},{12,16},{16,20},{20,24},{24,28},{1,5},{5,9},{9,... | collective-permute-start | bytes 589832 | tf_op jit(solution)/shard_map/while/body/eval_jaxpr/ppermute | solution.py:29
  317.8 4.5 %collective-permute-start = (bf16[2,384,128]{2,1,0:T(8,128)(2,1)S(1)}, bf16[2,384,128]{2,1,0:T(8,128)(2,1)S(1)}, u32[]{:S(2)}, u32[]{:S(2)}) collective-permute-start(bf16[2,384,128]{2,1,0:T(8,128)(2,1)S(1)} %convert_element_type.50), channel_id=1, source_target_pairs={{4,0},{8,4},{12,8},{16,12},{20,16},{24,20},{28,24},{5,1},{9,5},{13... | collective-permute-start | bytes 589832 | tf_op jit(solution)/shard_map/while/body/eval_jaxpr/ppermute | solution.py:29
  319.1 24.9 %collective-permute-start.1 = (bf16[2,384,128]{2,1,0:T(8,128)(2,1)S(1)}, bf16[2,384,128]{2,1,0:T(8,128)(2,1)S(1)}, u32[]{:S(2)}, u32[]{:S(2)}) collective-permute-start(bf16[2,384,128]{2,1,0:T(8,128)(2,1)S(1)} %convert_element_type.51), channel_id=1, source_target_pairs={{0,4},{4,8},{8,12},{12,16},{16,20},{20,24},{24,28},{1,5},{5,9},{9,... | collective-permute-start | bytes 589832 | tf_op jit(solution)/shard_map/while/body/eval_jaxpr/ppermute | solution.py:29
  (23 other events, 554.2 us)
where the time goes:
time: 368 us; the launch traced here: 365 us
  blocking collectives  256 us (70%)
  starting transfers between devices  53.7 us (15%)
  matrix products  34.4 us (9%)
  waiting for transfers between devices  13.6 us (4%)
  other arithmetic  4.26 us (1%)
    all_gather x7, blocking collectives, pair_turn(): lax.all_gather(below, 'lat', axis=1, tiled=True)  129 us
    all_gather x7, blocking collectives, pair_turn(): lax.all_gather(above, 'lat', axis=1, tiled=True)  127 us
    dot_general x28, matrix products, add_block(): jnp.dot(columns, piece[part], preferred_element_type=jnp.float32)  34.4 us
    ppermute x14, starting transfers between devices, shifted(): return lax.ppermute(block, axis, route)  31.3 us
    ppermute x4, starting transfers between devices, padded_2(): lax.ppermute(lax.slice_in_dim(block, block.shape[dim] - width, None, axis...  17.1 us
    ppermute x4, waiting for transfers between devices, padded_2(): lax.ppermute(lax.slice_in_dim(block, 0, width, axis=dim), axis, backward)  12.5 us
  transfers between devices with their start and end apart: 22, of which 4 were waited for; matrix products, arithmetic and copies ran while one was open for 7% of the time, Pallas kernels for 0%

commit v1 on v0

v1 whole, which is shorter than its diff:
```python
import functools

import jax
import jax.numpy as jnp
from jax import lax
from jax.experimental import pallas as pl
from jax.experimental.pallas import tpu as pltpu
from jax.sharding import PartitionSpec as P

RELAX = 4
HALO = 8
MESH = pl.DeviceIdType.MESH

relax_weight = 0.8
damping = 0.5


def relaxed(source, wave_sq, inside):
    rows, lanes = wave_sq.shape
    lane = lax.broadcasted_iota(jnp.int32, (rows, lanes), 1)
    first, last = lane == 0, lane == lanes - 1
    diag_real = 4.0 - wave_sq
    diag_imag = damping * wave_sq
    scale = jnp.where(inside, relax_weight, 0.0) / (diag_real * diag_real + diag_imag * diag_imag)
    inverse_real = diag_real * scale
    inverse_imag = -diag_imag * scale

    def beside(field):
        total = pltpu.roll(field, 1, 0) + pltpu.roll(field, rows - 1, 0)
        total = total + jnp.where(first, 0.0, pltpu.roll(field, 1, 1))
        return total + jnp.where(last, 0.0, pltpu.roll(field, lanes - 1, 1))

    real = source[0] * inverse_real - source[1] * inverse_imag
    imag = source[0] * inverse_imag + source[1] * inverse_real
    for _ in range(RELAX - 1):
        res_real = source[0] - (diag_real * real - diag_imag * imag - beside(real))
        res_imag = source[1] - (diag_real * imag + diag_imag * real - beside(imag))
        real = real + res_real * inverse_real - res_imag * inverse_imag
        imag = imag + res_real * inverse_imag + res_imag * inverse_real
    return real, imag


def kernel(layers, slabs, source, wave, green_down, green_up, down, up, green, held, ready, trace, wide_source,
           wide_wave, green_sem, halo_send, halo_recv, send_sem, recv_sem):
    me_layer, me_slab = lax.axis_index("layer"), lax.axis_index("lat")
    slab = trace.shape[1]
    half = slab * slabs // 2

    loads = [
        pltpu.make_async_copy(block, green.at[way], green_sem.at[way])
        for way, block in enumerate((green_down, green_up))
    ]
    for load in loads:
        load.start()

    barrier = pltpu.get_barrier_semaphore()
    me = me_layer * slabs + me_slab

    def greet(other, carry):
        @pl.when(other != me)
        def _():
            pl.semaphore_signal(barrier, inc=1, device_id=(other // slabs, other % slabs), device_id_type=MESH)

        return carry

    lax.fori_loop(0, layers * slabs, greet, 0)
    wide_source[:, HALO : HALO + slab] = source[...]
    wide_wave[HALO : HALO + slab] = wave[...]
    pl.semaphore_wait(barrier, layers * slabs - 1)

    def halo_copies(side):
        rows = pl.ds(slab - HALO, HALO) if side == 0 else pl.ds(0, HALO)
        lands = pl.ds(0, HALO) if side == 0 else pl.ds(HALO + slab, HALO)
        other = me_slab + 1 if side == 0 else me_slab - 1
        other = jnp.clip(other, 0, slabs - 1)
        return [
            pltpu.make_async_remote_copy(
                src_ref=src, dst_ref=dst, send_sem=halo_send.at[side, n], recv_sem=halo_recv.at[side, n],
                device_id=(me_layer, other), device_id_type=MESH,
            )
            for n, (src, dst) in enumerate(
                ((source.at[:, rows], wide_source.at[:, lands]), (wave.at[rows], wide_wave.at[lands]))
            )
        ]

    has_next, has_previous = me_slab < slabs - 1, me_slab > 0
    sends, receives = (has_next, has_previous), (has_previous, has_next)
    for side in range(2):
        @pl.when(sends[side])
        def _():
            for copy in halo_copies(side):
                copy.start()

        @pl.when(jnp.logical_not(receives[side]))
        def _():
            lands = pl.ds(0, HALO) if side == 0 else pl.ds(HALO + slab, HALO)
            wide_source[:, lands] = jnp.zeros((2, HALO, source.shape[2]), jnp.float32)
            wide_wave[lands] = jnp.ones((HALO, source.shape[2]), jnp.float32)

    for side in range(2):
        @pl.when(receives[side])
        def _():
            for copy in halo_copies(side):
                copy.wait_recv()

    row = lax.broadcasted_iota(jnp.int32, wide_wave.shape, 0) - HALO + me_slab * slab
    inside = jnp.logical_and(row >= 0, row < slab * slabs)
    field = relaxed(wide_source[...], wide_wave[...], inside)
    for part in range(2):
        trace[part] = field[part][HALO : HALO + slab]

    def turn_copy(way, target, slot, semaphore):
        here = pl.ds(pl.multiple_of(slot * slab, 16), slab)
        step = jnp.where(way == 0, 1, -1)
        return pltpu.make_async_remote_copy(
            src_ref=ready.at[way], dst_ref=held.at[way, :, here, :],
            send_sem=send_sem.at[way, semaphore], recv_sem=recv_sem.at[way, slot],
            device_id=(jnp.clip(me_layer + step, 0, layers - 1), target), device_id_type=MESH,
        )

    def put(way, part, value):
        ready[way, part] = value.astype(jnp.bfloat16)

        @pl.when(way == 0)
        def _():
            down[part] = value

        @pl.when(way == 1)
        def _():
            up[part] = value

    def turn(order, carry):
        way = jnp.where(me_layer < layers // 2, order, 1 - order)
        place = jnp.where(way == 0, me_layer, layers - 1 - me_layer)

        @pl.when(place == 0)
        def _():
            for part in range(2):
                put(way, part, trace[part])

        @pl.when(place > 0)
        def _():
            pltpu.make_async_copy(green_down, green.at[way], green_sem.at[way]).wait()
            near = me_slab // (slabs // 2)
            totals = [trace[0], trace[1]]
            for turn_half in range(2):
                now = near if turn_half == 0 else 1 - near
                for n in range(slabs // 2):
                    turn_copy(way, me_slab, now * (slabs // 2) + n, 0).wait_recv()
                for part in range(2):
                    for cut in range(2):
                        columns = pl.ds(pl.multiple_of(cut * 2 * half + now * half, 128), half)
                        totals[part] = totals[part] + jnp.dot(
                            green[way, pl.ds(part * slab, slab), columns],
                            held[way, cut, pl.ds(pl.multiple_of(now * half, 16), half), :],
                            preferred_element_type=jnp.float32,
                        )
            for part in range(2):
                put(way, part, totals[part])

        @pl.when(place < layers - 1)
        def _():
            for target in range(slabs):
                turn_copy(way, target, me_slab, target).start()

        return carry

    lax.fori_loop(0, 2, turn, 0)

    for way in range(2):
        place = me_layer if way == 0 else layers - 1 - me_layer

        @pl.when(place == 0)
        def _():
            loads[way].wait()

        @pl.when(place < layers - 1)
        def _():
            for target in range(slabs):
                turn_copy(way, target, me_slab, target).wait_send()

    for side in range(2):
        @pl.when(sends[side])
        def _():
            for copy in halo_copies(side):
                copy.wait_send()


def local(source, wavenumber, green_down, green_up):
    layers, slabs = lax.axis_size("layer"), lax.axis_size("lat")
    _, parts, slab, lanes = source.shape
    width = slab * slabs
    shape = jax.ShapeDtypeStruct((parts, slab, lanes), jnp.float32)
    vmem = pl.BlockSpec(memory_space=pltpu.VMEM)
    anywhere = pl.BlockSpec(memory_space=pl.ANY)
    down, up = pl.pallas_call(
        functools.partial(kernel, layers, slabs),
        out_shape=(shape, shape),
        in_specs=[vmem, vmem, anywhere, anywhere],
        out_specs=(vmem, vmem),
        scratch_shapes=[
            pltpu.VMEM((2, parts * slab, parts * width), jnp.bfloat16),
            pltpu.VMEM((2, parts, width, lanes), jnp.bfloat16),
            pltpu.VMEM((2, parts, slab, lanes), jnp.bfloat16),
            pltpu.VMEM((parts, slab, lanes), jnp.float32),
            pltpu.VMEM((parts, slab + 2 * HALO, lanes), jnp.float32),
            pltpu.VMEM((slab + 2 * HALO, lanes), jnp.float32),
            pltpu.SemaphoreType.DMA((2,)),
            pltpu.SemaphoreType.DMA((2, 2)),
            pltpu.SemaphoreType.DMA((2, 2)),
            pltpu.SemaphoreType.DMA((2, slabs)),
            pltpu.SemaphoreType.DMA((2, slabs)),
        ],
        compiler_params=pltpu.CompilerParams(
            collective_id=0, has_side_effects=True, vmem_limit_bytes=32 * 1024 * 1024
        ),
    )(
        source[0],
        wavenumber[0],
        green_down.reshape(parts * slab, parts * width),
        green_up.reshape(parts * slab, parts * width),
    )
    return down[None], up[None]


def solution(mesh):
    return jax.shard_map(
        local,
        mesh=mesh,
        in_specs=(
            P("layer", None, "lat", None),
            P("layer", "lat", None),
            P("layer", None, "lat", None),
            P("layer", None, "lat", None),
        ),
        out_specs=(P("layer", None, "lat", None), P("layer", None, "lat", None)),
        check_vma=False,
    )
```

time: 368 us -> 99 us (0.27)
  blocking collectives: 256 us -> 0 us
  Pallas kernels: 0 us -> 89.6 us
  starting transfers between devices: 53.7 us -> 0 us
  matrix products: 34.4 us -> 0 us
  waiting for transfers between devices: 13.6 us -> 0 us
  local copies, waits for them, and re-layouts: 1.24 us -> 8.08 us
  other arithmetic: 4.26 us -> 0 us
    all_gather x14 -> x0, blocking collectives: 256 us -> none  [the longest x7 129 us: pair_turn(): lax.all_gather(below, 'lat', axis=1, tiled=True)]
    pallas_call x0 -> x1, Pallas kernels: none -> 89.6 us  [local(): pl.pallas_call(functools.partial(kernel, layers, slabs), out_shape=(shape...]
    ppermute x22 -> x0, starting transfers between devices: 53.7 us -> none  [the longest x14 31.3 us: shifted(): return lax.ppermute(block, axis, route)]
    dot_general x28 -> x0, matrix products: 34.4 us -> none  [add_block(): jnp.dot(columns, piece[part], preferred_element_type=jnp.float32)]
    ppermute x22 -> x0, waiting for transfers between devices: 13.6 us -> none  [the longest x4 12.5 us: padded_2(): lax.ppermute(lax.slice_in_dim(block, 0, width, axis=dim), axis, backward)]
    unnamed x10, local copies, waits for them, and re-layouts: 0.93 us -> 8.08 us
  transfers between devices with their start and end apart: 22 -> 0, of which waited for: 4 -> 0; matrix products, arithmetic and copies ran while one was open for 7% -> 0% of each run, Pallas kernels for 0% -> 0%
where the time goes in v1:
time: 99 us; the launch traced here: 98.3 us
  Pallas kernels  89.6 us (91%)
  local copies, waits for them, and re-layouts  8.08 us (8%)
    pallas_call x1, Pallas kernels, local(): pl.pallas_call(functools.partial(kernel, layers, slabs), out_shape=(shape...  89.6 us
    unnamed x10, local copies, waits for them, and re-layouts  8.08 us

profile of v1, /device:TPU:0, one launch (start us, length us, event | category | flops | bytes accessed | tf_op | source)
XLA Modules:
  0.0 98.3 jit_solution(2498825552571883057)
XLA Ops:
  0.6 0.0 copy-start
  0.6 2.3 %copy-done = bf16[1,2,384,3072]{3,2,1,0:T(8,128)(2,1)S(1)} copy-done((bf16[1,2,384,3072]{3,2,1,0:T(8,128)(2,1)S(1)}, bf16[1,2,384,3072]{3,2,1,0:T(8,128)(2,1)}, u32[]{:S(2)}) %copy-start) | copy-done | bytes 4718616
  3.0 0.0 copy-start.1
  3.0 2.3 %copy-done.1 = bf16[1,2,384,3072]{3,2,1,0:T(8,128)(2,1)S(1)} copy-done((bf16[1,2,384,3072]{3,2,1,0:T(8,128)(2,1)S(1)}, bf16[1,2,384,3072]{3,2,1,0:T(8,128)(2,1)}, u32[]{:S(2)}) %copy-start.1) | copy-done | bytes 4718616
  5.3 0.0 copy-start.2
  5.3 1.0 %copy-done.2 = f32[1,2,384,128]{3,2,1,0:T(8,128)S(1)} copy-done((f32[1,2,384,128]{3,2,1,0:T(8,128)S(1)}, f32[1,2,384,128]{3,2,1,0:T(8,128)}, u32[]{:S(2)}) %copy-start.2) | copy-done | bytes 393240
  6.3 0.0 copy-start.3
  6.3 0.9 copy-done.3
  7.2 89.6 %shard_map.59 = (f32[2,384,128]{2,1,0:T(8,128)S(1)}, f32[2,384,128]{2,1,0:T(8,128)S(1)}) custom-call(f32[2,384,128]{2,1,0:T(8,128)S(1)} %bitcast.8, f32[384,128]{1,0:T(8,128)S(1)} %bitcast.11, bf16[768,3072]{1,0:T(8,128)(2,1)S(1)} %bitcast.6, bf16[768,3072]{1,0:T(8,128)(2,1)S(1)} %bitcast.7), custom_call_target="tpu_custom_call" | custom-call | tf_op jit(solution)/shard_map/pallas_call | solution.py:196
  96.8 0.7 copy.8
  97.6 0.7 copy.9
Async XLA Ops:
  0.6 2.3 %copy-start = (bf16[1,2,384,3072]{3,2,1,0:T(8,128)(2,1)S(1)}, bf16[1,2,384,3072]{3,2,1,0:T(8,128)(2,1)}, u32[]{:S(2)}) copy-start(bf16[1,2,384,3072]{3,2,1,0:T(8,128)(2,1)} %param.6) | copy-start | bytes 14155780
  3.0 2.3 %copy-start.1 = (bf16[1,2,384,3072]{3,2,1,0:T(8,128)(2,1)S(1)}, bf16[1,2,384,3072]{3,2,1,0:T(8,128)(2,1)}, u32[]{:S(2)}) copy-start(bf16[1,2,384,3072]{3,2,1,0:T(8,128)(2,1)} %param.7) | copy-start | bytes 14155780
  5.3 1.0 %copy-start.2 = (f32[1,2,384,128]{3,2,1,0:T(8,128)S(1)}, f32[1,2,384,128]{3,2,1,0:T(8,128)}, u32[]{:S(2)}) copy-start(f32[1,2,384,128]{3,2,1,0:T(8,128)} %param.4) | copy-start | bytes 1179652
  6.3 0.9 copy-start.3

commit v2 on v1

--- a/solution.py
+++ b/solution.py
@@ -9,6 +9,7 @@
 
 RELAX = 4
 HALO = 8
+CHUNKS = 2
 MESH = pl.DeviceIdType.MESH
 
 relax_weight = 0.8
@@ -41,17 +42,27 @@
 
 
 def kernel(layers, slabs, source, wave, green_down, green_up, down, up, green, held, ready, trace, wide_source,
-           wide_wave, green_sem, halo_send, halo_recv, send_sem, recv_sem):
+           wide_wave, load_sem, halo_send, halo_recv, send_sem, recv_sem):
     me_layer, me_slab = lax.axis_index("layer"), lax.axis_index("lat")
     slab = trace.shape[1]
     half = slab * slabs // 2
+    lanes = trace.shape[2]
+    chunk_lanes = lanes // CHUNKS
+    middle = pl.ds(HALO, slab)
 
     loads = [
-        pltpu.make_async_copy(block, green.at[way], green_sem.at[way])
-        for way, block in enumerate((green_down, green_up))
+        pltpu.make_async_copy(src, dst, load_sem.at[n])
+        for n, (src, dst) in enumerate(
+            (
+                (green_down, green.at[0]),
+                (green_up, green.at[1]),
+                (source, wide_source.at[:, middle]),
+                (wave, wide_wave.at[middle]),
+            )
+        )
     ]
-    for load in loads:
-        load.start()
+    for n in (2, 3, 0, 1):
+        loads[n].start()
 
     barrier = pltpu.get_barrier_semaphore()
     me = me_layer * slabs + me_slab
@@ -64,8 +75,6 @@
         return carry
 
     lax.fori_loop(0, layers * slabs, greet, 0)
-    wide_source[:, HALO : HALO + slab] = source[...]
-    wide_wave[HALO : HALO + slab] = wave[...]
     pl.semaphore_wait(barrier, layers * slabs - 1)
 
     def halo_copies(side):
@@ -97,6 +106,8 @@
             wide_source[:, lands] = jnp.zeros((2, HALO, source.shape[2]), jnp.float32)
             wide_wave[lands] = jnp.ones((HALO, source.shape[2]), jnp.float32)
 
+    for n in (2, 3):
+        loads[n].wait()
     for side in range(2):
         @pl.when(receives[side])
         def _():
@@ -109,25 +120,38 @@
     for part in range(2):
         trace[part] = field[part][HALO : HALO + slab]
 
-    def turn_copy(way, target, slot, semaphore):
+    lane = lax.broadcasted_iota(jnp.int32, (slab, lanes), 1)
+
+    def push(way, chunk, target, slot):
         here = pl.ds(pl.multiple_of(slot * slab, 16), slab)
         step = jnp.where(way == 0, 1, -1)
         return pltpu.make_async_remote_copy(
-            src_ref=ready.at[way], dst_ref=held.at[way, :, here, :],
-            send_sem=send_sem.at[way, semaphore], recv_sem=recv_sem.at[way, slot],
+            src_ref=ready.at[way, chunk], dst_ref=held.at[way, chunk, here, :],
+            send_sem=send_sem.at[way, chunk, target], recv_sem=recv_sem.at[way, chunk, slot],
             device_id=(jnp.clip(me_layer + step, 0, layers - 1), target), device_id_type=MESH,
         )
 
-    def put(way, part, value):
-        ready[way, part] = value.astype(jnp.bfloat16)
-
-        @pl.when(way == 0)
-        def _():
-            down[part] = value
-
-        @pl.when(way == 1)
-        def _():
-            up[part] = value
+    def others_first():
+        return [lax.rem(me_slab + n, slabs) for n in range(1, slabs + 1)]
+
+    def put(way, chunk, place, value):
+        mine = lane // chunk_lanes == chunk
+        packed = jnp.where(mine, value[0], pltpu.roll(value[1], chunk_lanes, 1))
+        ready[way, chunk] = packed.astype(jnp.bfloat16)
+
+        @pl.when(place < layers - 1)
+        def _():
+            if chunk > 0:
+                for target in others_first():
+                    push(way, chunk - 1, target, me_slab).wait_send()
+            for target in others_first():
+                push(way, chunk, target, me_slab).start()
+
+        for out, here in ((down, way == 0), (up, way == 1)):
+            @pl.when(here)
+            def _():
+                for part in range(2):
+                    out[part] = value[part] if chunk == 0 else jnp.where(mine, value[part], out[part])
 
     def turn(order, carry):
         way = jnp.where(me_layer < layers // 2, order, 1 - order)
@@ -135,33 +159,35 @@
 
         @pl.when(place == 0)
         def _():
-            for part in range(2):
-                put(way, part, trace[part])
+            for chunk in range(CHUNKS):
+                put(way, chunk, place, (trace[0], trace[1]))
 
         @pl.when(place > 0)
         def _():
-            pltpu.make_async_copy(green_down, green.at[way], green_sem.at[way]).wait()
+            pltpu.make_async_copy(green_down, green.at[way], load_sem.at[way]).wait()
             near = me_slab // (slabs // 2)
-            totals = [trace[0], trace[1]]
-            for turn_half in range(2):
-                now = near if turn_half == 0 else 1 - near
-                for n in range(slabs // 2):
-                    turn_copy(way, me_slab, now * (slabs // 2) + n, 0).wait_recv()
-                for part in range(2):
-                    for cut in range(2):
-                        columns = pl.ds(pl.multiple_of(cut * 2 * half + now * half, 128), half)
-                        totals[part] = totals[part] + jnp.dot(
-                            green[way, pl.ds(part * slab, slab), columns],
-                            held[way, cut, pl.ds(pl.multiple_of(now * half, 16), half), :],
-                            preferred_element_type=jnp.float32,
-                        )
-            for part in range(2):
-                put(way, part, totals[part])
-
-        @pl.when(place < layers - 1)
-        def _():
-            for target in range(slabs):
-                turn_copy(way, target, me_slab, target).start()
+            for chunk in range(CHUNKS):
+                totals = [[None, None], [None, None]]
+                for turn_half in range(2):
+                    now = near if turn_half == 0 else 1 - near
+                    for n in range(slabs // 2):
+                        push(way, chunk, me_slab, now * (slabs // 2) + n).wait_recv()
+                    block = held[way, chunk, pl.ds(pl.multiple_of(now * half, 16), half), :]
+                    for part in range(2):
+                        for cut in range(2):
+                            columns = pl.ds(pl.multiple_of(cut * 2 * half + now * half, 128), half)
+                            product = jnp.dot(
+                                green[way, pl.ds(part * slab, slab), columns], block,
+                                preferred_element_type=jnp.float32,
+                            )
+                            if turn_half == 0:
+                                totals[part][cut] = product
+                            else:
+                                totals[part][cut] = totals[part][cut] + product
+                value = [
+                    trace[part] + totals[part][0] + pltpu.roll(totals[part][1], chunk_lanes, 1) for part in range(2)
+                ]
+                put(way, chunk, place, value)
 
         return carry
 
@@ -176,14 +202,34 @@
 
         @pl.when(place < layers - 1)
         def _():
-            for target in range(slabs):
-                turn_copy(way, target, me_slab, target).wait_send()
+            for target in others_first():
+                push(way, CHUNKS - 1, target, me_slab).wait_send()
 
     for side in range(2):
         @pl.when(sends[side])
         def _():
             for copy in halo_copies(side):
                 copy.wait_send()
+
+
+def written(down, up, down_out, up_out, held, sem):
+    loads = [
+        pltpu.make_async_copy(src.at[part], held.at[way, part], sem.at[0, way, part])
+        for way, src in enumerate((down, up))
+        for part in range(2)
+    ]
+    stores = [
+        pltpu.make_async_copy(held.at[way, part], dst.at[part], sem.at[1, way, part])
+        for way, dst in enumerate((down_out, up_out))
+        for part in range(2)
+    ]
+    for load in loads:
+        load.start()
+    for load, store in zip(loads, stores):
+        load.wait()
+        store.start()
+    for store in stores:
+        store.wait()
 
 
 def local(source, wavenumber, green_down, green_up):
@@ -192,27 +238,28 @@
     width = slab * slabs
     shape = jax.ShapeDtypeStruct((parts, slab, lanes), jnp.float32)
     vmem = pl.BlockSpec(memory_space=pltpu.VMEM)
-    anywhere = pl.BlockSpec(memory_space=pl.ANY)
+    hbm = pl.BlockSpec(memory_space=pltpu.HBM)
+    per_slab = pltpu.SemaphoreType.DMA((2, CHUNKS, slabs))
     down, up = pl.pallas_call(
         functools.partial(kernel, layers, slabs),
         out_shape=(shape, shape),
-        in_specs=[vmem, vmem, anywhere, anywhere],
+        in_specs=[hbm] * 4,
         out_specs=(vmem, vmem),
         scratch_shapes=[
             pltpu.VMEM((2, parts * slab, parts * width), jnp.bfloat16),
-            pltpu.VMEM((2, parts, width, lanes), jnp.bfloat16),
-            pltpu.VMEM((2, parts, slab, lanes), jnp.bfloat16),
+            pltpu.VMEM((2, CHUNKS, width, lanes), jnp.bfloat16),
+            pltpu.VMEM((2, CHUNKS, slab, lanes), jnp.bfloat16),
             pltpu.VMEM((parts, slab, lanes), jnp.float32),
             pltpu.VMEM((parts, slab + 2 * HALO, lanes), jnp.float32),
             pltpu.VMEM((slab + 2 * HALO, lanes), jnp.float32),
-            pltpu.SemaphoreType.DMA((2,)),
+            pltpu.SemaphoreType.DMA((4,)),
             pltpu.SemaphoreType.DMA((2, 2)),
             pltpu.SemaphoreType.DMA((2, 2)),
-            pltpu.SemaphoreType.DMA((2, slabs)),
-            pltpu.SemaphoreType.DMA((2, slabs)),
+            per_slab,
+            per_slab,
         ],
         compiler_params=pltpu.CompilerParams(
-            collective_id=0, has_side_effects=True, vmem_limit_bytes=32 * 1024 * 1024
+            collective_id=0, has_side_effects=True, vmem_limit_bytes=60 * 1024 * 1024
         ),
     )(
         source[0],
@@ -220,6 +267,17 @@
         green_down.reshape(parts * slab, parts * width),
         green_up.reshape(parts * slab, parts * width),
     )
+    down, up = pl.pallas_call(
+        written,
+        out_shape=(shape, shape),
+        in_specs=[hbm] * 2,
+        out_specs=(hbm, hbm),
+        scratch_shapes=[
+            pltpu.VMEM((2, parts, slab, lanes), jnp.float32),
+            pltpu.SemaphoreType.DMA((2, 2, parts)),
+        ],
+        compiler_params=pltpu.CompilerParams(vmem_limit_bytes=60 * 1024 * 1024),
+    )(down, up)
     return down[None], up[None]
 
 

time: 99 us -> 87.5 us (0.88)
  local copies, waits for them, and re-layouts: 8.08 us -> 0 us
  Pallas kernels: 89.6 us -> 86 us
    unnamed x10 -> x0, local copies, waits for them, and re-layouts: 8.08 us -> none
    pallas_call x1, Pallas kernels: 89.6 us -> 84 us  [local(): pl.pallas_call(functools.partial(kernel, layers, slabs), out_shape=(shape...]
    pallas_call x0 -> x1, Pallas kernels: none -> 1.97 us  [local(): pl.pallas_call(written, out_shape=(shape, shape), in_specs=[hbm] * 2, out...]
where the time goes in v2:
time: 87.5 us; the launch traced here: 86.6 us
  Pallas kernels  86 us (98%)
    pallas_call x1, Pallas kernels, local(): pl.pallas_call(functools.partial(kernel, layers, slabs), out_shape=(shape...  84 us
    pallas_call x1, Pallas kernels, local(): pl.pallas_call(written, out_shape=(shape, shape), in_specs=[hbm] * 2, out...  1.97 us

profile of v2, /device:TPU:0, one launch (start us, length us, event | category | flops | bytes accessed | tf_op | source)
XLA Modules:
  0.0 86.6 jit_solution(525292620865555516)
XLA Ops:
  0.6 84.0 %shard_map.59 = (f32[2,384,128]{2,1,0:T(8,128)}, f32[2,384,128]{2,1,0:T(8,128)}) custom-call(f32[2,384,128]{2,1,0:T(8,128)} %bitcast.8, f32[384,128]{1,0:T(8,128)} %bitcast.9, bf16[768,3072]{1,0:T(8,128)(2,1)} %bitcast.6, bf16[768,3072]{1,0:T(8,128)(2,1)} %bitcast.7), custom_call_target="tpu_custom_call" | custom-call | tf_op jit(solution)/shard_map/pallas_call | solution.py:243
  84.7 2.0 %shard_map.60 = (f32[2,384,128]{2,1,0:T(8,128)}, f32[2,384,128]{2,1,0:T(8,128)}) custom-call(f32[2,384,128]{2,1,0:T(8,128)} %get-tuple-element.6.down, f32[2,384,128]{2,1,0:T(8,128)} %get-tuple-element.7.up), custom_call_target="tpu_custom_call" | custom-call | tf_op jit(solution)/shard_map/pallas_call | solution.py:270

commit v3 on v2

--- a/solution.py
+++ b/solution.py
@@ -10,6 +10,7 @@
 RELAX = 4
 HALO = 8
 CHUNKS = 2
+FAR, NEAR = 2, 1
 MESH = pl.DeviceIdType.MESH
 
 relax_weight = 0.8
@@ -42,7 +43,7 @@
 
 
 def kernel(layers, slabs, source, wave, green_down, green_up, down, up, green, held, ready, trace, wide_source,
-           wide_wave, load_sem, halo_send, halo_recv, send_sem, recv_sem):
+           wide_wave, load_sem, halo_send, halo_recv, send_sem, recv_sem, forward_send):
     me_layer, me_slab = lax.axis_index("layer"), lax.axis_index("lat")
     slab = trace.shape[1]
     half = slab * slabs // 2
@@ -131,8 +132,40 @@
             device_id=(jnp.clip(me_layer + step, 0, layers - 1), target), device_id_type=MESH,
         )
 
-    def others_first():
-        return [lax.rem(me_slab + n, slabs) for n in range(1, slabs + 1)]
+    def forward(way, chunk, slot, toward):
+        here = pl.ds(pl.multiple_of(jnp.clip(slot, 0, slabs - 1) * slab, 16), slab)
+        index = jnp.clip(slot, 0, slabs - 1)
+        return pltpu.make_async_remote_copy(
+            src_ref=held.at[way, chunk, here, :], dst_ref=held.at[way, chunk, here, :],
+            send_sem=forward_send.at[way, chunk, index], recv_sem=recv_sem.at[way, chunk, index],
+            device_id=(me_layer, jnp.clip(toward, 0, slabs - 1)), device_id_type=MESH,
+        )
+
+    def within(place):
+        return jnp.logical_and(place >= 0, place < slabs)
+
+    def reach(layer, other):
+        return jnp.where(layer // 2 == other // 2, FAR, NEAR)
+
+    def each_push(way, chunk, act):
+        limit = reach(me_layer, jnp.where(way == 0, me_layer + 1, me_layer - 1))
+        for distance in range(FAR, -1, -1):
+            for sign in (1, -1)[: 1 if distance == 0 else 2]:
+                target = me_slab + sign * distance
+
+                @pl.when(jnp.logical_and(within(target), distance <= limit))
+                def _():
+                    act(push(way, chunk, jnp.clip(target, 0, slabs - 1), me_slab))
+
+    def each_forward(way, chunk, act):
+        limit = reach(me_layer, jnp.where(way == 0, me_layer - 1, me_layer + 1))
+        for distance in range(1, slabs):
+            for sign in (1, -1):
+                slot, toward = me_slab - sign * distance, me_slab + sign
+
+                @pl.when(jnp.logical_and(jnp.logical_and(within(slot), within(toward)), distance >= limit))
+                def _():
+                    act(forward(way, chunk, slot, toward))
 
     def put(way, chunk, place, value):
         mine = lane // chunk_lanes == chunk
@@ -142,10 +175,8 @@
         @pl.when(place < layers - 1)
         def _():
             if chunk > 0:
-                for target in others_first():
-                    push(way, chunk - 1, target, me_slab).wait_send()
-            for target in others_first():
-                push(way, chunk, target, me_slab).start()
+                each_push(way, chunk - 1, lambda copy: copy.wait_send())
+            each_push(way, chunk, lambda copy: copy.start())
 
         for out, here in ((down, way == 0), (up, way == 1)):
             @pl.when(here)
@@ -166,12 +197,26 @@
         def _():
             pltpu.make_async_copy(green_down, green.at[way], load_sem.at[way]).wait()
             near = me_slab // (slabs // 2)
+            limit = reach(me_layer, jnp.where(way == 0, me_layer - 1, me_layer + 1))
+
+            def hand_on(copy):
+                copy.wait_recv()
+                copy.start()
+
             for chunk in range(CHUNKS):
+                each_forward(way, chunk, hand_on)
                 totals = [[None, None], [None, None]]
                 for turn_half in range(2):
                     now = near if turn_half == 0 else 1 - near
                     for n in range(slabs // 2):
-                        push(way, chunk, me_slab, now * (slabs // 2) + n).wait_recv()
+                        slot = now * (slabs // 2) + n
+                        toward = jnp.where(slot < me_slab, me_slab + 1, me_slab - 1)
+                        handed_on = jnp.logical_and(jnp.where(slot < me_slab, me_slab - slot, slot - me_slab) >= limit, within(toward))
+
+                        @pl.when(jnp.logical_not(handed_on))
+                        def _():
+                            push(way, chunk, me_slab, slot).wait_recv()
+
                     block = held[way, chunk, pl.ds(pl.multiple_of(now * half, 16), half), :]
                     for part in range(2):
                         for cut in range(2):
@@ -202,8 +247,12 @@
 
         @pl.when(place < layers - 1)
         def _():
-            for target in others_first():
-                push(way, CHUNKS - 1, target, me_slab).wait_send()
+            each_push(way, CHUNKS - 1, lambda copy: copy.wait_send())
+
+        @pl.when(place > 0)
+        def _():
+            for chunk in range(CHUNKS):
+                each_forward(way, chunk, lambda copy: copy.wait_send())
 
     for side in range(2):
         @pl.when(sends[side])
@@ -257,6 +306,7 @@
             pltpu.SemaphoreType.DMA((2, 2)),
             per_slab,
             per_slab,
+            per_slab,
         ],
         compiler_params=pltpu.CompilerParams(
             collective_id=0, has_side_effects=True, vmem_limit_bytes=60 * 1024 * 1024

time: 87.5 us -> 98.1 us (1.12)
  Pallas kernels: 86 us -> 97.3 us
    pallas_call x1, Pallas kernels: 84 us -> 95.3 us  [local(): pl.pallas_call(functools.partial(kernel, layers, slabs), out_shape=(shape...]
where the time goes in v3:
time: 98.1 us; the launch traced here: 97.9 us
  Pallas kernels  97.3 us (99%)
    pallas_call x1, Pallas kernels, local(): pl.pallas_call(functools.partial(kernel, layers, slabs), out_shape=(shape...  95.3 us
    pallas_call x1, Pallas kernels, local(): pl.pallas_call(written, out_shape=(shape, shape), in_specs=[hbm] * 2, out...  1.97 us

profile of v3, /device:TPU:0, one launch (start us, length us, event | category | flops | bytes accessed | tf_op | source)
XLA Modules:
  0.0 97.9 jit_solution(15629521716595906103)
XLA Ops:
  0.6 95.3 %shard_map.59 = (f32[2,384,128]{2,1,0:T(8,128)}, f32[2,384,128]{2,1,0:T(8,128)}) custom-call(f32[2,384,128]{2,1,0:T(8,128)} %bitcast.8, f32[384,128]{1,0:T(8,128)} %bitcast.9, bf16[768,3072]{1,0:T(8,128)(2,1)} %bitcast.6, bf16[768,3072]{1,0:T(8,128)(2,1)} %bitcast.7), custom_call_target="tpu_custom_call" | custom-call | tf_op jit(solution)/shard_map/pallas_call | solution.py:292
  95.9 2.0 %shard_map.60 = (f32[2,384,128]{2,1,0:T(8,128)}, f32[2,384,128]{2,1,0:T(8,128)}) custom-call(f32[2,384,128]{2,1,0:T(8,128)} %get-tuple-element.6.down, f32[2,384,128]{2,1,0:T(8,128)} %get-tuple-element.7.up), custom_call_target="tpu_custom_call" | custom-call | tf_op jit(solution)/shard_map/pallas_call | solution.py:320
